TPU v7x, 512 devices: a whole 4x8x8 slice. The times are simulated.
512 devices in a mesh: seq: 64 (over y, z_hi, core), head: 8 (over x, z_lo).
Axes of the slice: x: 4, y: 8, z: 8 (z_hi: 4, z_lo: 2; z = z_hi * 2 + z_lo), core: 2. Of those that a mesh axis runs over, the one named last changes fastest.
Arguments:
- query_rows: bfloat16 [32768, 4096], P(('seq', 'head')), may hold values from -18 to 18
- key_rows: bfloat16 [32768, 4096], P(('seq', 'head')), may hold values from -18 to 18
- value_rows: bfloat16 [32768, 4096], P(('seq', 'head')), may hold values from -6 to 6
- doc_first: int32 [64], replicated, may hold values from 0 to 63, as said below
Outputs:
- attended: bfloat16 [32768, 4096], P(('seq', 'head'))
- log_totals: float32 [32, 32768], P('head', 'seq')
Inputs may be any that keep to these rules, and one draw needn't show every extreme that they name: The blocks form documents of consecutive blocks: doc_first never falls, doc_first[doc_first[b]] = doc_first[b], b - 8 < doc_first[b] <= b, and some document holds exactly 8 blocks.
All inputs are finite; a program needn't handle non-finite values.
Results may differ from a plain program's by a relative error of at most 0.0059.
Values may be sent and summed in bfloat16 or wider, within the bound.
A program may use at most 64 MiB of HBM per device.

v0:
```python
import math

import jax
import jax.numpy as jnp
from jax import lax
from jax.sharding import PartitionSpec as P

HD = 128


def from_behind(value, axis, steps):
    count = lax.axis_size(axis)
    first, last = (max(0, -steps), min(count, count - steps))
    return lax.ppermute(value, axis, [(source, source + steps) for source in range(first, last)])


def attend_tile(queries, key_block, value_block, causal):
    scaling = 1.0 / math.sqrt(HD)
    query_count = queries.shape[0]
    head_count = queries.shape[1] // HD
    query_heads = queries.reshape(query_count, head_count, HD)
    key_heads = key_block.reshape(key_block.shape[0], head_count, HD)
    value_heads = value_block.reshape(value_block.shape[0], head_count, HD)
    scores = (
        jnp.einsum("qhd,khd->hqk", query_heads, key_heads, preferred_element_type=jnp.float32)
        * scaling
    )
    if causal is not None:
        scores = jnp.where(causal[None], scores, -jnp.inf)
    maxima = jnp.max(scores, axis=-1)
    weights = jnp.exp(scores - maxima[..., None]).astype(jnp.bfloat16)
    totals = jnp.sum(weights.astype(jnp.float32), axis=-1)
    partial_value = jnp.einsum(
        "hqk,khd->hqd", weights, value_heads, preferred_element_type=jnp.float32
    )
    return (maxima, totals, partial_value)


def combine(running, fresh):
    highest = jnp.maximum(running[0], fresh[0])
    old_scale = jnp.exp(running[0] - highest)
    new_scale = jnp.exp(fresh[0] - highest)
    return (
        highest,
        running[1] * old_scale + fresh[1] * new_scale,
        running[2] * old_scale[..., None] + fresh[2] * new_scale[..., None],
    )


def fold_block(active, running, queries, key_block, value_block):
    return lax.cond(
        active,
        lambda: combine(running, attend_tile(queries, key_block, value_block, None)),
        lambda: running,
    )


def cycle_step(step_index, cycle_keys, cycle_values, running, home_queries, backward):
    cycle_keys, cycle_values = from_behind((cycle_keys, cycle_values), "seq", 1)
    running = fold_block(step_index <= backward, running, home_queries, cycle_keys, cycle_values)
    return (cycle_keys, cycle_values, running)


def on_device(query_rows, key_rows, value_rows, doc_first):
    queries_here, keys_here, values_here = (
        lax.all_to_all(query_rows, "head", split_axis=1, concat_axis=0, tiled=True),
        lax.all_to_all(key_rows, "head", split_axis=1, concat_axis=0, tiled=True),
        lax.all_to_all(value_rows, "head", split_axis=1, concat_axis=0, tiled=True),
    )
    block_rows = queries_here.shape[0]
    cycle_size = lax.axis_size("seq")
    reach_steps = cycle_size // 8
    position = lax.axis_index("seq")
    backward = position - doc_first[position]
    indices = jnp.arange(block_rows, dtype=jnp.int32)
    causal = indices[:, None] >= indices[None, :]
    home = attend_tile(queries_here, keys_here, values_here, causal)

    def advance_home(step_index, carried):
        return cycle_step(step_index, carried[0], carried[1], carried[2], queries_here, backward)

    carried = lax.fori_loop(1, reach_steps, advance_home, (keys_here, values_here, home))
    home = carried[2]
    maxima, totals, partial_value = home
    output = (
        (partial_value / totals[..., None])
        .transpose(1, 0, 2)
        .reshape(block_rows, -1)
        .astype(jnp.bfloat16)
    )
    attended = lax.all_to_all(output, "head", split_axis=0, concat_axis=1, tiled=True)
    return (attended, maxima + jnp.log(totals))


def solution(mesh):
    in_specs = (P(("seq", "head"), None), P(("seq", "head"), None), P(("seq", "head"), None), P())
    out_specs = (P(("seq", "head"), None), P("head", "seq"))
    return jax.shard_map(
        on_device, mesh=mesh, in_specs=in_specs, out_specs=out_specs, check_vma=False
    )
```

profile of v0, /device:TPU:32, one launch (start us, length us, event | category | flops | bytes accessed | tf_op | source)
XLA Modules:
  0.0 295.7 jit_solution(1638507007296200379)
XLA Ops:
  0.6 1.9 copy.77
  2.6 6.1 %all-to-all-start.2 = ((bf16[64,8,512]{2,0,1:T(8,128)(2,1)}), bf16[64,8,512]{2,0,1:T(8,128)(2,1)S(1)}, u32[]{:S(2)}, u32[]{:S(2)}) async-start(bf16[64,8,512]{2,0,1:T(8,128)(2,1)} %bitcast.49), calls=%async_computation.2 | async-start | bytes 1048576 | tf_op jit(solution)/shard_map/all_to_all | solution.py:66
  8.7 1.9 copy.79
  10.6 8.2 %all-to-all-done.2 = bf16[64,8,512]{2,0,1:T(8,128)(2,1)S(1)} async-done(((bf16[64,8,512]{2,0,1:T(8,128)(2,1)}), bf16[64,8,512]{2,0,1:T(8,128)(2,1)S(1)}, u32[]{:S(2)}, u32[]{:S(2)}) %all-to-all-start.2) | async-done | bytes 524320 | tf_op jit(solution)/shard_map/all_to_all | solution.py:66
  18.8 3.5 %all-to-all-start = ((bf16[64,8,512]{2,0,1:T(8,128)(2,1)}), bf16[64,8,512]{2,0,1:T(8,128)(2,1)S(1)}, u32[]{:S(2)}, u32[]{:S(2)}) async-start(bf16[64,8,512]{2,0,1:T(8,128)(2,1)} %bitcast.51), calls=%async_computation | async-start | bytes 1048576 | tf_op jit(solution)/shard_map/all_to_all | solution.py:67
  23.2 8.2 %all-to-all-done = bf16[64,8,512]{2,0,1:T(8,128)(2,1)S(1)} async-done(((bf16[64,8,512]{2,0,1:T(8,128)(2,1)}), bf16[64,8,512]{2,0,1:T(8,128)(2,1)S(1)}, u32[]{:S(2)}, u32[]{:S(2)}) %all-to-all-start) | async-done | bytes 524320 | tf_op jit(solution)/shard_map/all_to_all | solution.py:67
  31.4 4.2 %all-to-all-start.1 = ((bf16[64,8,512]{2,0,1:T(8,128)(2,1)}), bf16[64,8,512]{2,0,1:T(8,128)(2,1)}, u32[]{:S(2)}, u32[]{:S(2)}) async-start(bf16[64,8,512]{2,0,1:T(8,128)(2,1)} %bitcast.50), calls=%async_computation.1 | async-start | bytes 1048576 | tf_op jit(solution)/shard_map/all_to_all | solution.py:68
  37.2 7.1 %all-to-all-done.1 = bf16[64,8,512]{2,0,1:T(8,128)(2,1)} async-done(((bf16[64,8,512]{2,0,1:T(8,128)(2,1)}), bf16[64,8,512]{2,0,1:T(8,128)(2,1)}, u32[]{:S(2)}, u32[]{:S(2)}) %all-to-all-start.1) | async-done | bytes 524320 | tf_op jit(solution)/shard_map/all_to_all | solution.py:68
  44.3 2.0 reshape.59
  49.5 231.5 %while.21 = (s32[]{:T(128)}, bf16[512,512]{1,0:T(8,128)(2,1)S(1)}, bf16[512,512]{1,0:T(8,128)(2,1)}, f32[4,512]{1,0:T(4,128)S(1)}, f32[4,512]{1,0:T(4,128)S(1)},...) while((s32[]{:T(128)}, bf16[512,512]{1,0:T(8,128)(2,1)S(1)}, ...), condition=%wide.region_7.8_spmd, body=%wide.region_2.7_spmd.sunk | while | flops 548151296 | bytes 22659364 | solution.py:82
  49.5 1.9 collective-permute-start
  51.5 6.2 %collective-permute-start.1 = (bf16[512,512]{1,0:T(8,128)(2,1)}, bf16[512,512]{1,0:T(8,128)(2,1)S(1)}, u32[]{:S(2)}, u32[]{:S(2)}) collective-permute-start(bf16[512,512]{1,0:T(8,128)(2,1)} %get-tuple-element.275), channel_id=1, source_target_pairs={{0,8},{8,16},{16,24},{24,32},{32,40},{40,48},{48,56},{56,64},{64,7... | collective-permute-start | bytes 1572872 | tf_op jit(solution)/shard_map/while/body/eval_jaxpr/ppermute | solution.py:14
  57.7 12.5 %collective-permute-done = bf16[512,512]{1,0:T(8,128)(2,1)S(1)} collective-permute-done((bf16[512,512]{1,0:T(8,128)(2,1)S(1)}, bf16[512,512]{1,0:T(8,128)(2,1)S(1)}, u32[]{:S(2)}, u32[]{:S(2)}) %collective-permute-start) | collective-permute-done | bytes 524320 | tf_op jit(solution)/shard_map/while/body/eval_jaxpr/ppermute | solution.py:14
  70.2 10.3 %collective-permute-done.1 = bf16[512,512]{1,0:T(8,128)(2,1)S(1)} collective-permute-done((bf16[512,512]{1,0:T(8,128)(2,1)}, bf16[512,512]{1,0:T(8,128)(2,1)S(1)}, u32[]{:S(2)}, u32[]{:S(2)}) %collective-permute-start.1) | collective-permute-done | bytes 524320 | tf_op jit(solution)/shard_map/while/body/eval_jaxpr/ppermute | solution.py:14
  80.5 3.2 %conditional.2 = ((f32[4,512]{1,0:T(4,128)S(1)}, f32[4,512]{1,0:T(4,128)S(1)}, f32[4,512,128]{2,1,0:T(8,128)S(1)})) conditional(s32[]{:T(128)} %convert_element_type.48, (f32[4,512]{1,0:T(4,128)S(1)}, f32[4,512]{1,0:T(4,128)S(1)}, f32[4,512,128]{2,1,0:T(8,128)S(1)}) %tuple.46, (bf16[512,512]{1,0:T(8,128)(2,1)S(1)}, bf16[512,512]{1,0:T(8,128)(2,1)S(1)}, ...), branch_computations={%region_3.3_spmd, %region_4.6_spmd} | conditional | flops 548151296 | bytes 16367648 | solution.py:51
  84.6 1.9 collective-permute-start
  86.5 3.5 %collective-permute-start.1 = (bf16[512,512]{1,0:T(8,128)(2,1)}, bf16[512,512]{1,0:T(8,128)(2,1)S(1)}, u32[]{:S(2)}, u32[]{:S(2)}) collective-permute-start(bf16[512,512]{1,0:T(8,128)(2,1)} %get-tuple-element.275), channel_id=1, source_target_pairs={{0,8},{8,16},{16,24},{24,32},{32,40},{40,48},{48,56},{56,64},{64,7... | collective-permute-start | bytes 1572872 | tf_op jit(solution)/shard_map/while/body/eval_jaxpr/ppermute | solution.py:14
  90.0 15.2 %collective-permute-done = bf16[512,512]{1,0:T(8,128)(2,1)S(1)} collective-permute-done((bf16[512,512]{1,0:T(8,128)(2,1)S(1)}, bf16[512,512]{1,0:T(8,128)(2,1)S(1)}, u32[]{:S(2)}, u32[]{:S(2)}) %collective-permute-start) | collective-permute-done | bytes 524320 | tf_op jit(solution)/shard_map/while/body/eval_jaxpr/ppermute | solution.py:14
  105.2 9.9 %collective-permute-done.1 = bf16[512,512]{1,0:T(8,128)(2,1)S(1)} collective-permute-done((bf16[512,512]{1,0:T(8,128)(2,1)}, bf16[512,512]{1,0:T(8,128)(2,1)S(1)}, u32[]{:S(2)}, u32[]{:S(2)}) %collective-permute-start.1) | collective-permute-done | bytes 524320 | tf_op jit(solution)/shard_map/while/body/eval_jaxpr/ppermute | solution.py:14
  115.1 3.2 %conditional.2 = ((f32[4,512]{1,0:T(4,128)S(1)}, f32[4,512]{1,0:T(4,128)S(1)}, f32[4,512,128]{2,1,0:T(8,128)S(1)})) conditional(s32[]{:T(128)} %convert_element_type.48, (f32[4,512]{1,0:T(4,128)S(1)}, f32[4,512]{1,0:T(4,128)S(1)}, f32[4,512,128]{2,1,0:T(8,128)S(1)}) %tuple.46, (bf16[512,512]{1,0:T(8,128)(2,1)S(1)}, bf16[512,512]{1,0:T(8,128)(2,1)S(1)}, ...), branch_computations={%region_3.3_spmd, %region_4.6_spmd} | conditional | flops 548151296 | bytes 16367648 | solution.py:51
  116.5 1.8 fusion
  119.2 1.9 collective-permute-start
  121.1 1.9 collective-permute-start.1
  123.0 16.8 %collective-permute-done = bf16[512,512]{1,0:T(8,128)(2,1)S(1)} collective-permute-done((bf16[512,512]{1,0:T(8,128)(2,1)S(1)}, bf16[512,512]{1,0:T(8,128)(2,1)S(1)}, u32[]{:S(2)}, u32[]{:S(2)}) %collective-permute-start) | collective-permute-done | bytes 524320 | tf_op jit(solution)/shard_map/while/body/eval_jaxpr/ppermute | solution.py:14
  139.8 9.4 %collective-permute-done.1 = bf16[512,512]{1,0:T(8,128)(2,1)S(1)} collective-permute-done((bf16[512,512]{1,0:T(8,128)(2,1)}, bf16[512,512]{1,0:T(8,128)(2,1)S(1)}, u32[]{:S(2)}, u32[]{:S(2)}) %collective-permute-start.1) | collective-permute-done | bytes 524320 | tf_op jit(solution)/shard_map/while/body/eval_jaxpr/ppermute | solution.py:14
  149.2 3.2 %conditional.2 = ((f32[4,512]{1,0:T(4,128)S(1)}, f32[4,512]{1,0:T(4,128)S(1)}, f32[4,512,128]{2,1,0:T(8,128)S(1)})) conditional(s32[]{:T(128)} %convert_element_type.48, (f32[4,512]{1,0:T(4,128)S(1)}, f32[4,512]{1,0:T(4,128)S(1)}, f32[4,512,128]{2,1,0:T(8,128)S(1)}) %tuple.46, (bf16[512,512]{1,0:T(8,128)(2,1)S(1)}, bf16[512,512]{1,0:T(8,128)(2,1)S(1)}, ...), branch_computations={%region_3.3_spmd, %region_4.6_spmd} | conditional | flops 548151296 | bytes 16367648 | solution.py:51
  153.3 1.9 collective-permute-start
  155.3 1.9 collective-permute-start.1
  157.2 16.8 %collective-permute-done = bf16[512,512]{1,0:T(8,128)(2,1)S(1)} collective-permute-done((bf16[512,512]{1,0:T(8,128)(2,1)S(1)}, bf16[512,512]{1,0:T(8,128)(2,1)S(1)}, u32[]{:S(2)}, u32[]{:S(2)}) %collective-permute-start) | collective-permute-done | bytes 524320 | tf_op jit(solution)/shard_map/while/body/eval_jaxpr/ppermute | solution.py:14
  174.0 9.7 %collective-permute-done.1 = bf16[512,512]{1,0:T(8,128)(2,1)S(1)} collective-permute-done((bf16[512,512]{1,0:T(8,128)(2,1)}, bf16[512,512]{1,0:T(8,128)(2,1)S(1)}, u32[]{:S(2)}, u32[]{:S(2)}) %collective-permute-start.1) | collective-permute-done | bytes 524320 | tf_op jit(solution)/shard_map/while/body/eval_jaxpr/ppermute | solution.py:14
  183.7 3.2 %conditional.2 = ((f32[4,512]{1,0:T(4,128)S(1)}, f32[4,512]{1,0:T(4,128)S(1)}, f32[4,512,128]{2,1,0:T(8,128)S(1)})) conditional(s32[]{:T(128)} %convert_element_type.48, (f32[4,512]{1,0:T(4,128)S(1)}, f32[4,512]{1,0:T(4,128)S(1)}, f32[4,512,128]{2,1,0:T(8,128)S(1)}) %tuple.46, (bf16[512,512]{1,0:T(8,128)(2,1)S(1)}, bf16[512,512]{1,0:T(8,128)(2,1)S(1)}, ...), branch_computations={%region_3.3_spmd, %region_4.6_spmd} | conditional | flops 548151296 | bytes 16367648 | solution.py:51
  185.1 1.8 fusion
  187.8 1.9 collective-permute-start
  189.7 1.9 collective-permute-start.1
  191.6 16.8 %collective-permute-done = bf16[512,512]{1,0:T(8,128)(2,1)S(1)} collective-permute-done((bf16[512,512]{1,0:T(8,128)(2,1)S(1)}, bf16[512,512]{1,0:T(8,128)(2,1)S(1)}, u32[]{:S(2)}, u32[]{:S(2)}) %collective-permute-start) | collective-permute-done | bytes 524320 | tf_op jit(solution)/shard_map/while/body/eval_jaxpr/ppermute | solution.py:14
  208.4 7.9 %collective-permute-done.1 = bf16[512,512]{1,0:T(8,128)(2,1)S(1)} collective-permute-done((bf16[512,512]{1,0:T(8,128)(2,1)}, bf16[512,512]{1,0:T(8,128)(2,1)S(1)}, u32[]{:S(2)}, u32[]{:S(2)}) %collective-permute-start.1) | collective-permute-done | bytes 524320 | tf_op jit(solution)/shard_map/while/body/eval_jaxpr/ppermute | solution.py:14
  216.3 3.2 %conditional.2 = ((f32[4,512]{1,0:T(4,128)S(1)}, f32[4,512]{1,0:T(4,128)S(1)}, f32[4,512,128]{2,1,0:T(8,128)S(1)})) conditional(s32[]{:T(128)} %convert_element_type.48, (f32[4,512]{1,0:T(4,128)S(1)}, f32[4,512]{1,0:T(4,128)S(1)}, f32[4,512,128]{2,1,0:T(8,128)S(1)}) %tuple.46, (bf16[512,512]{1,0:T(8,128)(2,1)S(1)}, bf16[512,512]{1,0:T(8,128)(2,1)S(1)}, ...), branch_computations={%region_3.3_spmd, %region_4.6_spmd} | conditional | flops 548151296 | bytes 16367648 | solution.py:51
  217.8 1.8 fusion
  220.4 1.9 collective-permute-start
  222.4 1.9 collective-permute-start.1
  224.3 16.8 %collective-permute-done = bf16[512,512]{1,0:T(8,128)(2,1)S(1)} collective-permute-done((bf16[512,512]{1,0:T(8,128)(2,1)S(1)}, bf16[512,512]{1,0:T(8,128)(2,1)S(1)}, u32[]{:S(2)}, u32[]{:S(2)}) %collective-permute-start) | collective-permute-done | bytes 524320 | tf_op jit(solution)/shard_map/while/body/eval_jaxpr/ppermute | solution.py:14
  241.1 9.0 %collective-permute-done.1 = bf16[512,512]{1,0:T(8,128)(2,1)S(1)} collective-permute-done((bf16[512,512]{1,0:T(8,128)(2,1)}, bf16[512,512]{1,0:T(8,128)(2,1)S(1)}, u32[]{:S(2)}, u32[]{:S(2)}) %collective-permute-start.1) | collective-permute-done | bytes 524320 | tf_op jit(solution)/shard_map/while/body/eval_jaxpr/ppermute | solution.py:14
  251.0 1.9 collective-permute-start
  252.9 1.9 collective-permute-start.1
  254.9 16.8 %collective-permute-done = bf16[512,512]{1,0:T(8,128)(2,1)S(1)} collective-permute-done((bf16[512,512]{1,0:T(8,128)(2,1)S(1)}, bf16[512,512]{1,0:T(8,128)(2,1)S(1)}, u32[]{:S(2)}, u32[]{:S(2)}) %collective-permute-start) | collective-permute-done | bytes 524320 | tf_op jit(solution)/shard_map/while/body/eval_jaxpr/ppermute | solution.py:14
  271.7 8.5 %collective-permute-done.1 = bf16[512,512]{1,0:T(8,128)(2,1)S(1)} collective-permute-done((bf16[512,512]{1,0:T(8,128)(2,1)}, bf16[512,512]{1,0:T(8,128)(2,1)S(1)}, u32[]{:S(2)}, u32[]{:S(2)}) %collective-permute-start.1) | collective-permute-done | bytes 524320 | tf_op jit(solution)/shard_map/while/body/eval_jaxpr/ppermute | solution.py:14
  282.7 3.5 %all-to-all-start.3 = ((bf16[8,64,512]{2,1,0:T(8,128)(2,1)}), bf16[8,64,512]{2,1,0:T(8,128)(2,1)S(1)}, u32[]{:S(2)}, u32[]{:S(2)}) async-start(bf16[8,64,512]{2,1,0:T(8,128)(2,1)} %convert_element_type.33), calls=%async_computation.3 | async-start | bytes 1048576 | tf_op jit(solution)/shard_map/all_to_all | solution.py:91
  286.9 8.0 %all-to-all-done.3 = bf16[8,64,512]{2,1,0:T(8,128)(2,1)S(1)} async-done(((bf16[8,64,512]{2,1,0:T(8,128)(2,1)}), bf16[8,64,512]{2,1,0:T(8,128)(2,1)S(1)}, u32[]{:S(2)}, u32[]{:S(2)}) %all-to-all-start.3) | async-done | bytes 524320 | tf_op jit(solution)/shard_map/all_to_all | solution.py:91
  (52 shorter events, 24.9 us)
Async XLA Ops:
  0.6 21.7 %copy-start = (bf16[64,4096]{1,0:T(8,128)(2,1)S(1)}, bf16[64,4096]{1,0:T(8,128)(2,1)}, u32[]{:S(2)}) copy-start(bf16[64,4096]{1,0:T(8,128)(2,1)} %param.10) | copy-start | bytes 1572868
  0.6 34.9 %copy-start.2 = (s32[64]{0:T(128)S(1)}, s32[64]{0:T(128)}, u32[]{:S(2)}) copy-start(s32[64]{0:T(128)} %param.11) | copy-start | bytes 772
  2.6 16.2 %all-to-all-start.2 = ((bf16[64,8,512]{2,0,1:T(8,128)(2,1)}), bf16[64,8,512]{2,0,1:T(8,128)(2,1)S(1)}, u32[]{:S(2)}, u32[]{:S(2)}) async-start(bf16[64,8,512]{2,0,1:T(8,128)(2,1)} %bitcast.49), calls=%async_computation.2 | async-start | bytes 1048576 | tf_op jit(solution)/shard_map/all_to_all | solution.py:66
  18.8 12.6 %all-to-all-start = ((bf16[64,8,512]{2,0,1:T(8,128)(2,1)}), bf16[64,8,512]{2,0,1:T(8,128)(2,1)S(1)}, u32[]{:S(2)}, u32[]{:S(2)}) async-start(bf16[64,8,512]{2,0,1:T(8,128)(2,1)} %bitcast.51), calls=%async_computation | async-start | bytes 1048576 | tf_op jit(solution)/shard_map/all_to_all | solution.py:67
  31.4 12.9 %all-to-all-start.1 = ((bf16[64,8,512]{2,0,1:T(8,128)(2,1)}), bf16[64,8,512]{2,0,1:T(8,128)(2,1)}, u32[]{:S(2)}, u32[]{:S(2)}) async-start(bf16[64,8,512]{2,0,1:T(8,128)(2,1)} %bitcast.50), calls=%async_computation.1 | async-start | bytes 1048576 | tf_op jit(solution)/shard_map/all_to_all | solution.py:68
  46.2 1.8 copy-start.1
  49.5 20.7 %collective-permute-start = (bf16[512,512]{1,0:T(8,128)(2,1)S(1)}, bf16[512,512]{1,0:T(8,128)(2,1)S(1)}, u32[]{:S(2)}, u32[]{:S(2)}) collective-permute-start(bf16[512,512]{1,0:T(8,128)(2,1)S(1)} %get-tuple-element.274), channel_id=1, source_target_pairs={{0,8},{8,16},{16,24},{24,32},{32,40},{40,48},{48,56},{56,64},{64,7... | collective-permute-start | bytes 1572872 | tf_op jit(solution)/shard_map/while/body/eval_jaxpr/ppermute | solution.py:14
  51.5 29.0 %collective-permute-start.1 = (bf16[512,512]{1,0:T(8,128)(2,1)}, bf16[512,512]{1,0:T(8,128)(2,1)S(1)}, u32[]{:S(2)}, u32[]{:S(2)}) collective-permute-start(bf16[512,512]{1,0:T(8,128)(2,1)} %get-tuple-element.275), channel_id=1, source_target_pairs={{0,8},{8,16},{16,24},{24,32},{32,40},{40,48},{48,56},{56,64},{64,7... | collective-permute-start | bytes 1572872 | tf_op jit(solution)/shard_map/while/body/eval_jaxpr/ppermute | solution.py:14
  84.6 20.7 %collective-permute-start = (bf16[512,512]{1,0:T(8,128)(2,1)S(1)}, bf16[512,512]{1,0:T(8,128)(2,1)S(1)}, u32[]{:S(2)}, u32[]{:S(2)}) collective-permute-start(bf16[512,512]{1,0:T(8,128)(2,1)S(1)} %get-tuple-element.274), channel_id=1, source_target_pairs={{0,8},{8,16},{16,24},{24,32},{32,40},{40,48},{48,56},{56,64},{64,7... | collective-permute-start | bytes 1572872 | tf_op jit(solution)/shard_map/while/body/eval_jaxpr/ppermute | solution.py:14
  86.5 28.6 %collective-permute-start.1 = (bf16[512,512]{1,0:T(8,128)(2,1)}, bf16[512,512]{1,0:T(8,128)(2,1)S(1)}, u32[]{:S(2)}, u32[]{:S(2)}) collective-permute-start(bf16[512,512]{1,0:T(8,128)(2,1)} %get-tuple-element.275), channel_id=1, source_target_pairs={{0,8},{8,16},{16,24},{24,32},{32,40},{40,48},{48,56},{56,64},{64,7... | collective-permute-start | bytes 1572872 | tf_op jit(solution)/shard_map/while/body/eval_jaxpr/ppermute | solution.py:14
  119.2 20.7 %collective-permute-start = (bf16[512,512]{1,0:T(8,128)(2,1)S(1)}, bf16[512,512]{1,0:T(8,128)(2,1)S(1)}, u32[]{:S(2)}, u32[]{:S(2)}) collective-permute-start(bf16[512,512]{1,0:T(8,128)(2,1)S(1)} %get-tuple-element.274), channel_id=1, source_target_pairs={{0,8},{8,16},{16,24},{24,32},{32,40},{40,48},{48,56},{56,64},{64,7... | collective-permute-start | bytes 1572872 | tf_op jit(solution)/shard_map/while/body/eval_jaxpr/ppermute | solution.py:14
  121.1 28.1 %collective-permute-start.1 = (bf16[512,512]{1,0:T(8,128)(2,1)}, bf16[512,512]{1,0:T(8,128)(2,1)S(1)}, u32[]{:S(2)}, u32[]{:S(2)}) collective-permute-start(bf16[512,512]{1,0:T(8,128)(2,1)} %get-tuple-element.275), channel_id=1, source_target_pairs={{0,8},{8,16},{16,24},{24,32},{32,40},{40,48},{48,56},{56,64},{64,7... | collective-permute-start | bytes 1572872 | tf_op jit(solution)/shard_map/while/body/eval_jaxpr/ppermute | solution.py:14
  153.3 20.7 %collective-permute-start = (bf16[512,512]{1,0:T(8,128)(2,1)S(1)}, bf16[512,512]{1,0:T(8,128)(2,1)S(1)}, u32[]{:S(2)}, u32[]{:S(2)}) collective-permute-start(bf16[512,512]{1,0:T(8,128)(2,1)S(1)} %get-tuple-element.274), channel_id=1, source_target_pairs={{0,8},{8,16},{16,24},{24,32},{32,40},{40,48},{48,56},{56,64},{64,7... | collective-permute-start | bytes 1572872 | tf_op jit(solution)/shard_map/while/body/eval_jaxpr/ppermute | solution.py:14
  155.3 28.4 %collective-permute-start.1 = (bf16[512,512]{1,0:T(8,128)(2,1)}, bf16[512,512]{1,0:T(8,128)(2,1)S(1)}, u32[]{:S(2)}, u32[]{:S(2)}) collective-permute-start(bf16[512,512]{1,0:T(8,128)(2,1)} %get-tuple-element.275), channel_id=1, source_target_pairs={{0,8},{8,16},{16,24},{24,32},{32,40},{40,48},{48,56},{56,64},{64,7... | collective-permute-start | bytes 1572872 | tf_op jit(solution)/shard_map/while/body/eval_jaxpr/ppermute | solution.py:14
  187.8 20.7 %collective-permute-start = (bf16[512,512]{1,0:T(8,128)(2,1)S(1)}, bf16[512,512]{1,0:T(8,128)(2,1)S(1)}, u32[]{:S(2)}, u32[]{:S(2)}) collective-permute-start(bf16[512,512]{1,0:T(8,128)(2,1)S(1)} %get-tuple-element.274), channel_id=1, source_target_pairs={{0,8},{8,16},{16,24},{24,32},{32,40},{40,48},{48,56},{56,64},{64,7... | collective-permute-start | bytes 1572872 | tf_op jit(solution)/shard_map/while/body/eval_jaxpr/ppermute | solution.py:14
  189.7 26.7 %collective-permute-start.1 = (bf16[512,512]{1,0:T(8,128)(2,1)}, bf16[512,512]{1,0:T(8,128)(2,1)S(1)}, u32[]{:S(2)}, u32[]{:S(2)}) collective-permute-start(bf16[512,512]{1,0:T(8,128)(2,1)} %get-tuple-element.275), channel_id=1, source_target_pairs={{0,8},{8,16},{16,24},{24,32},{32,40},{40,48},{48,56},{56,64},{64,7... | collective-permute-start | bytes 1572872 | tf_op jit(solution)/shard_map/while/body/eval_jaxpr/ppermute | solution.py:14
  220.4 20.7 %collective-permute-start = (bf16[512,512]{1,0:T(8,128)(2,1)S(1)}, bf16[512,512]{1,0:T(8,128)(2,1)S(1)}, u32[]{:S(2)}, u32[]{:S(2)}) collective-permute-start(bf16[512,512]{1,0:T(8,128)(2,1)S(1)} %get-tuple-element.274), channel_id=1, source_target_pairs={{0,8},{8,16},{16,24},{24,32},{32,40},{40,48},{48,56},{56,64},{64,7... | collective-permute-start | bytes 1572872 | tf_op jit(solution)/shard_map/while/body/eval_jaxpr/ppermute | solution.py:14
  222.4 27.8 %collective-permute-start.1 = (bf16[512,512]{1,0:T(8,128)(2,1)}, bf16[512,512]{1,0:T(8,128)(2,1)S(1)}, u32[]{:S(2)}, u32[]{:S(2)}) collective-permute-start(bf16[512,512]{1,0:T(8,128)(2,1)} %get-tuple-element.275), channel_id=1, source_target_pairs={{0,8},{8,16},{16,24},{24,32},{32,40},{40,48},{48,56},{56,64},{64,7... | collective-permute-start | bytes 1572872 | tf_op jit(solution)/shard_map/while/body/eval_jaxpr/ppermute | solution.py:14
  251.0 20.7 %collective-permute-start = (bf16[512,512]{1,0:T(8,128)(2,1)S(1)}, bf16[512,512]{1,0:T(8,128)(2,1)S(1)}, u32[]{:S(2)}, u32[]{:S(2)}) collective-permute-start(bf16[512,512]{1,0:T(8,128)(2,1)S(1)} %get-tuple-element.274), channel_id=1, source_target_pairs={{0,8},{8,16},{16,24},{24,32},{32,40},{40,48},{48,56},{56,64},{64,7... | collective-permute-start | bytes 1572872 | tf_op jit(solution)/shard_map/while/body/eval_jaxpr/ppermute | solution.py:14
  252.9 27.2 %collective-permute-start.1 = (bf16[512,512]{1,0:T(8,128)(2,1)}, bf16[512,512]{1,0:T(8,128)(2,1)S(1)}, u32[]{:S(2)}, u32[]{:S(2)}) collective-permute-start(bf16[512,512]{1,0:T(8,128)(2,1)} %get-tuple-element.275), channel_id=1, source_target_pairs={{0,8},{8,16},{16,24},{24,32},{32,40},{40,48},{48,56},{56,64},{64,7... | collective-permute-start | bytes 1572872 | tf_op jit(solution)/shard_map/while/body/eval_jaxpr/ppermute | solution.py:14
  282.7 12.1 %all-to-all-start.3 = ((bf16[8,64,512]{2,1,0:T(8,128)(2,1)}), bf16[8,64,512]{2,1,0:T(8,128)(2,1)S(1)}, u32[]{:S(2)}, u32[]{:S(2)}) async-start(bf16[8,64,512]{2,1,0:T(8,128)(2,1)} %convert_element_type.33), calls=%async_computation.3 | async-start | bytes 1048576 | tf_op jit(solution)/shard_map/all_to_all | solution.py:91
where the time goes:
time: 297 us; the launch traced here: 296 us
  waiting for transfers between devices  208 us (70%)
  starting transfers between devices  50 us (17%)
  local copies, waits for them, and re-layouts  15.6 us (5%)
  matrix products  14.7 us (5%)
  other arithmetic  5.6 us (2%)
    ppermute x14, waiting for transfers between devices, from_behind(): lax.ppermute(value, axis, [(source, source + steps) for source in range(f...  176 us
    ppermute x14, starting transfers between devices, from_behind(): lax.ppermute(value, axis, [(source, source + steps) for source in range(f...  32.7 us
    dot_general x6, matrix products, attend_tile(): jnp.einsum('hqk,khd->hqd', weights, value_heads, preferred_element_type=j...  10.2 us
    all_to_all x1, waiting for transfers between devices, on_device(): lax.all_to_all(key_rows, 'head', split_axis=1, concat_axis=0, tiled=True)  8.25 us
    all_to_all x1, waiting for transfers between devices, on_device(): lax.all_to_all(query_rows, 'head', split_axis=1, concat_axis=0, tiled=True)  8.2 us
    all_to_all x1, waiting for transfers between devices, on_device(): lax.all_to_all(output, 'head', split_axis=0, concat_axis=1, tiled=True)  8.01 us
    all_to_all x1, waiting for transfers between devices, on_device(): lax.all_to_all(value_rows, 'head', split_axis=1, concat_axis=0, tiled=True)  7.1 us
    all_to_all x1, starting transfers between devices, on_device(): lax.all_to_all(query_rows, 'head', split_axis=1, concat_axis=0, tiled=True)  6.11 us
  transfers between devices with their start and end apart: 18, of which 18 were waited for; matrix products, arithmetic and copies ran while one was open for 1% of the time, Pallas kernels for 0%

commit v1 on v0

v1 whole, which is shorter than its diff:
```python
import functools
import math

import jax
import jax.numpy as jnp
from jax import lax
from jax.experimental import pallas as pl
from jax.experimental.pallas import tpu as pltpu
from jax.sharding import PartitionSpec as P

HD = 128
NX, NY, NZ = 4, 8, 8
PLANE = NX * NZ
ROWS = 64
BLOCK = 512
SUBS = BLOCK // ROWS
NB = 8
OWN = NB // 2
SCALE = 1.0 / math.sqrt(HD)
FLAGS = {"kv": True, "q": True, "fwd": True, "compute": True, "out": True}


def chip_device(y, x, z, core):
    return ((y * 4 + z // 2) * 2 + core, x * 2 + z % 2)


def shift(t):
    turn = t // 4
    far = 4 - (turn + 1) // 2
    dz = (8 + far * (2 * (turn % 2) - 1)) % 8
    return 3 - t % 4, dz


def attend_kernel(
    doc_ref, q_ref, k_ref, v_ref, out_ref, lse_ref,
    qbuf, kv, obuf, scores, lse_stage, lse_in,
    kv_send, kv_recv, q_send, q_recv, sib_send, sib_recv, fwd_send, fwd_recv,
    prev_send, prev_recv, o_send, o_recv, lse_send, lse_recv, local_sem,
):
    seq = lax.axis_index("seq")
    head = lax.axis_index("head")
    core = seq % 2
    y = seq // 8
    x = head // 2
    z = (seq // 2) % 4 * 2 + head % 2
    my_block = seq % 8
    my_sub = head
    my_head = x * 8 + z

    sibling = chip_device(y, x, z, 1 - core)
    ahead = chip_device((y + 1) % NY, x, z, core)
    behind = chip_device((y + NY - 1) % NY, x, z, core)

    def target(t):
        dx, dz = shift(t)
        tx, tz = (x + dx) % NX, (z + dz) % NZ
        return chip_device(y, tx, tz, core), tx * 8 + tz

    def source(t):
        dx, dz = shift(t)
        sx, sz = (x + NX - dx) % NX, (z + NZ - dz) % NZ
        return sz // 2, sx * 2 + sz % 2

    barrier = pltpu.get_barrier_semaphore()

    def greet(t, carry):
        pl.semaphore_signal(barrier, inc=1, device_id=target(t)[0], device_id_type=pl.DeviceIdType.MESH)
        return carry

    lax.fori_loop(0, PLANE - 1, greet, 0)
    for other in (sibling, ahead, behind):
        pl.semaphore_signal(barrier, inc=1, device_id=other, device_id_type=pl.DeviceIdType.MESH)
    pl.semaphore_wait(barrier, PLANE + 2)

    def columns(h):
        return pl.ds(pl.multiple_of(h * HD, HD), HD)

    def remote(src, dst, send_sem, recv_sem, device):
        return pltpu.make_async_remote_copy(
            src_ref=src, dst_ref=dst, send_sem=send_sem, recv_sem=recv_sem,
            device_id=device, device_id_type=pl.DeviceIdType.MESH,
        )

    if FLAGS["kv"]:
        def send_kv(t, carry):
            device, h = target(t)
            for which, ref in ((0, k_ref), (1, v_ref)):
                remote(ref.at[:, columns(h)], kv.at[1, my_block, my_sub, which],
                       kv_send.at[which], kv_recv.at[t], device).start()
            return carry

        lax.fori_loop(0, PLANE - 1, send_kv, 0)
        for which, ref in ((0, k_ref), (1, v_ref)):
            pltpu.make_async_copy(ref.at[:, columns(my_head)], kv.at[1, my_block, my_sub, which],
                                  local_sem.at[which]).start()
    if FLAGS["q"]:
        def send_q(t, carry):
            device, h = target(t)
            remote(q_ref.at[:, columns(h)], qbuf.at[my_block // 2, my_sub],
                   q_send, q_recv, device).start()
            return carry

        lax.fori_loop(0, PLANE - 1, send_q, 0)
        pltpu.make_async_copy(q_ref.at[:, columns(my_head)], qbuf.at[my_block // 2, my_sub],
                              local_sem.at[2]).start()

    def chunk(plane, zh, parity, sub):
        return kv.at[plane, 2 * zh + parity, sub]

    if FLAGS["kv"]:
        def pass_on(t, zh, sub):
            here = chunk(1, zh, core, sub)
            remote(here, here, sib_send, sib_recv, sibling).start()
            remote(here, chunk(0, zh, core, sub), fwd_send, fwd_recv.at[t], ahead).start()

        for which, ref in ((0, k_ref), (1, v_ref)):
            pltpu.make_async_copy(ref.at[:, columns(my_head)], kv.at[1, my_block, my_sub, which],
                                  local_sem.at[which]).wait()
        if FLAGS["fwd"]:
            pass_on(PLANE - 1, z // 2, my_sub)

        def take_kv(t, carry):
            zh, sub = source(t)
            here = chunk(1, zh, core, sub)
            remote(here, here, kv_send.at[0], kv_recv.at[t], sibling).wait_recv()
            if FLAGS["fwd"]:
                pass_on(t, zh, sub)
            return carry

        lax.fori_loop(0, PLANE - 1, take_kv, 0)

    if FLAGS["fwd"]:
        def take_prev(t, carry):
            zh, sub = source(t)
            here = chunk(0, zh, core, sub)
            remote(here, here, fwd_send, fwd_recv.at[t], sibling).wait_recv()
            remote(here, here, prev_send, prev_recv, sibling).start()
            return carry

        lax.fori_loop(0, PLANE, take_prev, 0)
        half = kv.at[0, pl.ds(0, OWN)]
        for send, recv in ((sib_send, sib_recv), (prev_send, prev_recv)):
            done = remote(half, half, send, recv, sibling)
            done.wait_send()
            done.wait_recv()
        remote(half, half, fwd_send, sib_recv, sibling).wait_send()

    if FLAGS["kv"]:
        for which, ref in ((0, k_ref), (1, v_ref)):
            most = ref.at[:, pl.ds(0, (PLANE - 1) * HD)]
            remote(most, most, kv_send.at[which], q_recv, sibling).wait_send()
    if FLAGS["q"]:
        pltpu.make_async_copy(q_ref.at[:, columns(my_head)], qbuf.at[my_block // 2, my_sub],
                              local_sem.at[2]).wait()
        most = q_ref.at[:, pl.ds(0, (PLANE - 1) * HD)]
        done = remote(most, most, q_send, q_recv, sibling)
        done.wait_send()
        done.wait_recv()

    row = lax.broadcasted_iota(jnp.int32, (BLOCK, BLOCK), 0)
    col = lax.broadcasted_iota(jnp.int32, (BLOCK, BLOCK), 1)

    def attend(zh, logs):
        i = 2 * zh + core
        first = doc_ref[y * NB + i]
        queries = qbuf[zh].reshape(BLOCK, HD)

        def where(step):
            j = (i + NB - step) % NB
            plane = (j <= i).astype(jnp.int32)
            visible = (y + plane - 1) * NB + j >= first
            return plane, j, visible

        def score(step):
            plane, j, visible = where(step)
            keys = kv[plane, j, :, 0].reshape(BLOCK, HD)
            return lax.dot_general(queries, keys, (((1,), (1,)), ((), ())),
                                   preferred_element_type=jnp.float32), visible

        def fold(s):
            return functools.reduce(jnp.maximum, [s[:, n * HD:(n + 1) * HD] for n in range(BLOCK // HD)])

        home, _ = score(0)
        home = jnp.where(row >= col, home, -jnp.inf)
        scores[0] = home

        def first_pass(step, peak):
            s, visible = score(step)
            scores[step] = s
            return jnp.maximum(peak, jnp.where(visible, fold(s), -jnp.inf))

        peak = lax.fori_loop(1, NB, first_pass, fold(home))
        top = jnp.max(peak, axis=1, keepdims=True)

        def weigh(step, carry):
            total, value = carry
            plane, j, visible = where(step)
            floor = jnp.where(visible, top, jnp.inf)
            w = jnp.exp((scores[step] - floor) * SCALE).astype(jnp.bfloat16)
            wide = w.astype(jnp.float32)
            total = total + functools.reduce(
                jnp.add, [wide[:, n * HD:(n + 1) * HD] for n in range(BLOCK // HD)])
            values = kv[plane, j, :, 1].reshape(BLOCK, HD)
            value = value + jnp.dot(w, values, preferred_element_type=jnp.float32)
            return total, value

        zero = jnp.zeros((BLOCK, HD), jnp.float32)
        total, value = lax.fori_loop(0, NB, weigh, (zero, zero))
        total = jnp.sum(total, axis=1, keepdims=True)
        obuf[zh] = (value / total).astype(jnp.bfloat16).reshape(SUBS, ROWS, HD)
        log_total = top * SCALE + jnp.log(total)
        lane = lax.broadcasted_iota(jnp.int32, (BLOCK, HD), 1)
        logs = jnp.where(lane == zh, log_total, logs)
        if FLAGS["out"]:
            send_out(zh)
        return logs

    def send_out(zh):
        def send(sub, carry):
            tx, tz = sub // 2, 2 * zh + sub % 2
            here = jnp.logical_and(tx == x, tz == z)

            @pl.when(jnp.logical_not(here))
            def _():
                remote(obuf.at[zh, sub], out_ref.at[:, columns(my_head)], o_send, o_recv,
                       chip_device(y, tx, tz, core)).start()

            @pl.when(here)
            def _():
                pltpu.make_async_copy(obuf.at[zh, sub], out_ref.at[:, columns(my_head)],
                                      local_sem.at[3]).start()
            return carry

        lax.fori_loop(0, SUBS, send, 0)

    logs = jnp.zeros((BLOCK, HD), jnp.float32)
    if FLAGS["compute"]:
        logs = lax.fori_loop(0, OWN, attend, logs)
    elif FLAGS["out"]:
        lax.fori_loop(0, OWN, lambda zh, c: (send_out(zh), c)[1], 0)

    if FLAGS["out"]:
        rows = jnp.transpose(logs)
        for zh in range(OWN):
            for n in range(BLOCK // HD):
                lse_stage[zh, n:n + 1, :] = rows[zh:zh + 1, n * HD:(n + 1) * HD]

        def send_logs(zh, carry):
            tz = 2 * zh + z // 4
            here = tz == z

            @pl.when(jnp.logical_not(here))
            def _():
                remote(lse_stage.at[zh], lse_in.at[z % 4], lse_send.at[zh], lse_recv.at[z % 4],
                       chip_device(y, x, tz, core)).start()

            @pl.when(here)
            def _():
                pltpu.make_async_copy(lse_stage.at[zh], lse_in.at[z % 4], local_sem.at[4]).start()
            return carry

        lax.fori_loop(0, OWN, send_logs, 0)

        def take_logs(r, carry):
            sz = (head % 2) * 4 + r
            here = sz == z

            @pl.when(jnp.logical_not(here))
            def _():
                remote(lse_stage.at[0], lse_in.at[r], lse_send.at[0], lse_recv.at[r], sibling).wait_recv()

            @pl.when(here)
            def _():
                pltpu.make_async_copy(lse_stage.at[0], lse_in.at[r], local_sem.at[4]).wait()
            return carry

        lax.fori_loop(0, 4, take_logs, 0)

        def drain_logs(zh, carry):
            @pl.when(2 * zh + z // 4 != z)
            def _():
                remote(lse_stage.at[zh], lse_in.at[0], lse_send.at[zh], lse_recv.at[0], sibling).wait_send()
            return carry

        lax.fori_loop(0, OWN, drain_logs, 0)
        for r in range(4):
            for n in range(BLOCK // HD):
                lse_ref[r:r + 1, n * HD:(n + 1) * HD] = lse_in[r, n:n + 1, :]

        pltpu.make_async_copy(obuf.at[0, 0], out_ref.at[:, columns(my_head)], local_sem.at[3]).wait()
        most = out_ref.at[:, pl.ds(0, (PLANE - 1) * HD)]
        done = remote(most, most, o_send, o_recv, sibling)
        done.wait_send()
        done.wait_recv()


def on_device(query_rows, key_rows, value_rows, doc_first):
    dma = pltpu.SemaphoreType.DMA
    any_space = pl.BlockSpec(memory_space=pl.ANY)
    return pl.pallas_call(
        attend_kernel,
        out_shape=(
            jax.ShapeDtypeStruct((ROWS, PLANE * HD), jnp.bfloat16),
            jax.ShapeDtypeStruct((4, BLOCK), jnp.float32),
        ),
        in_specs=[pl.BlockSpec(memory_space=pltpu.SMEM), any_space, any_space, any_space],
        out_specs=(any_space, pl.BlockSpec(memory_space=pltpu.VMEM)),
        scratch_shapes=[
            pltpu.VMEM((OWN, SUBS, ROWS, HD), jnp.bfloat16),
            pltpu.VMEM((2, NB, SUBS, 2, ROWS, HD), jnp.bfloat16),
            pltpu.VMEM((OWN, SUBS, ROWS, HD), jnp.bfloat16),
            pltpu.VMEM((NB, BLOCK, BLOCK), jnp.float32),
            pltpu.VMEM((OWN, 8, HD), jnp.float32),
            pltpu.VMEM((4, 8, HD), jnp.float32),
            dma((2,)), dma((PLANE,)), dma, dma, dma, dma, dma, dma((PLANE,)),
            dma, dma, dma, dma, dma((4,)), dma((4,)), dma((5,)),
        ],
        compiler_params=pltpu.CompilerParams(
            collective_id=0, has_side_effects=True, vmem_limit_bytes=48 * 1024 * 1024,
        ),
        cost_estimate=pl.CostEstimate(flops=17_000_000_000, bytes_accessed=4_000_000, transcendentals=8_400_000),
    )(doc_first, query_rows, key_rows, value_rows)


def solution(mesh):
    rows = P(("seq", "head"), None)
    return jax.shard_map(
        on_device, mesh=mesh, in_specs=(rows, rows, rows, P()),
        out_specs=(rows, P("head", "seq")), check_vma=False,
    )
```

time: 297 us -> 94.5 us (0.32)
  the two profiles are of different devices: /device:TPU:32 before, /device:TPU:1 now
where the time goes in v1:
time: 94.5 us; the launch traced here: 94.2 us
  Pallas kernels  88.4 us (94%)
  local copies, waits for them, and re-layouts  5.17 us (5%)
    pallas_call x1, Pallas kernels, on_device(): pl.pallas_call(attend_kernel, out_shape=(jax.ShapeDtypeStruct((ROWS, PLAN...  88.4 us
    unnamed x10, local copies, waits for them, and re-layouts  5.17 us

profile of v1, /device:TPU:1, one launch (start us, length us, event | category | flops | bytes accessed | tf_op | source)
XLA Modules:
  0.0 94.2 jit_solution(13914394500573294504)
XLA Ops:
  0.6 0.0 copy-start
  0.6 1.0 %copy-done = bf16[64,4096]{1,0:T(8,128)(2,1)S(1)} copy-done((bf16[64,4096]{1,0:T(8,128)(2,1)S(1)}, bf16[64,4096]{1,0:T(8,128)(2,1)}, u32[]{:S(2)}) %copy-start) | copy-done | bytes 524312
  1.7 0.0 copy-start.1
  1.7 1.0 %copy-done.1 = bf16[64,4096]{1,0:T(8,128)(2,1)S(1)} copy-done((bf16[64,4096]{1,0:T(8,128)(2,1)S(1)}, bf16[64,4096]{1,0:T(8,128)(2,1)}, u32[]{:S(2)}) %copy-start.1) | copy-done | bytes 524312
  2.7 0.0 copy-start.2
  2.7 1.0 %copy-done.2 = bf16[64,4096]{1,0:T(8,128)(2,1)S(1)} copy-done((bf16[64,4096]{1,0:T(8,128)(2,1)S(1)}, bf16[64,4096]{1,0:T(8,128)(2,1)}, u32[]{:S(2)}) %copy-start.2) | copy-done | bytes 524312
  3.8 0.0 copy-start.3
  3.8 0.7 copy-done.3
  4.4 88.4 %shard_map.59 = (bf16[64,4096]{1,0:T(8,128)(2,1)S(1)}, f32[4,512]{1,0:T(4,128)S(1)}) custom-call(s32[64]{0:T(128)S(1)} %copy-done.3, bf16[64,4096]{1,0:T(8,128)(2,1)S(1)} %copy-done, bf16[64,4096]{1,0:T(8,128)(2,1)S(1)} %copy-done.1, bf16[64,4096]{1,0:T(8,128)(2,1)S(1)} %copy-done.2), custom_call_target="tpu_custom_call" | custom-call | flops 16999999488 | bytes 4000000 | tf_op jit(solution)/shard_map/pallas_call | solution.py:300
  92.8 0.8 copy.8
  93.6 0.6 copy.9
Async XLA Ops:
  0.6 1.0 %copy-start = (bf16[64,4096]{1,0:T(8,128)(2,1)S(1)}, bf16[64,4096]{1,0:T(8,128)(2,1)}, u32[]{:S(2)}) copy-start(bf16[64,4096]{1,0:T(8,128)(2,1)} %q_ref.1) | copy-start | bytes 1572868
  1.7 1.0 %copy-start.1 = (bf16[64,4096]{1,0:T(8,128)(2,1)S(1)}, bf16[64,4096]{1,0:T(8,128)(2,1)}, u32[]{:S(2)}) copy-start(bf16[64,4096]{1,0:T(8,128)(2,1)} %k_ref.1) | copy-start | bytes 1572868
  2.7 1.0 %copy-start.2 = (bf16[64,4096]{1,0:T(8,128)(2,1)S(1)}, bf16[64,4096]{1,0:T(8,128)(2,1)}, u32[]{:S(2)}) copy-start(bf16[64,4096]{1,0:T(8,128)(2,1)} %v_ref.1) | copy-start | bytes 1572868
  3.8 0.7 copy-start.3

commit v2 on v1

--- a/solution.py
+++ b/solution.py
@@ -17,6 +17,10 @@
 NB = 8
 OWN = NB // 2
 SCALE = 1.0 / math.sqrt(HD)
+SCALE2 = SCALE * math.log2(math.e)
+TILE = 128
+TILES = BLOCK // TILE
+PART = 32
 FLAGS = {"kv": True, "q": True, "fwd": True, "compute": True, "out": True}
 
 
@@ -33,7 +37,7 @@
 
 def attend_kernel(
     doc_ref, q_ref, k_ref, v_ref, out_ref, lse_ref,
-    qbuf, kv, obuf, scores, lse_stage, lse_in,
+    docs, qbuf, kv, obuf, s0, s1, p0, p1, top0, top1, lse_stage, lse_in,
     kv_send, kv_recv, q_send, q_recv, sib_send, sib_recv, fwd_send, fwd_recv,
     prev_send, prev_recv, o_send, o_recv, lse_send, lse_recv, local_sem,
 ):
@@ -61,6 +65,8 @@
         sx, sz = (x + NX - dx) % NX, (z + NZ - dz) % NZ
         return sz // 2, sx * 2 + sz % 2
 
+    fetch_docs = pltpu.make_async_copy(doc_ref, docs, local_sem.at[2])
+    fetch_docs.start()
     barrier = pltpu.get_barrier_semaphore()
 
     def greet(t, carry):
@@ -97,12 +103,12 @@
         def send_q(t, carry):
             device, h = target(t)
             remote(q_ref.at[:, columns(h)], qbuf.at[my_block // 2, my_sub],
-                   q_send, q_recv, device).start()
+                   q_send, q_recv.at[my_block // 2], device).start()
             return carry
 
         lax.fori_loop(0, PLANE - 1, send_q, 0)
         pltpu.make_async_copy(q_ref.at[:, columns(my_head)], qbuf.at[my_block // 2, my_sub],
-                              local_sem.at[2]).start()
+                              q_recv.at[my_block // 2]).start()
 
     def chunk(plane, zh, parity, sub):
         return kv.at[plane, 2 * zh + parity, sub]
@@ -148,76 +154,83 @@
     if FLAGS["kv"]:
         for which, ref in ((0, k_ref), (1, v_ref)):
             most = ref.at[:, pl.ds(0, (PLANE - 1) * HD)]
-            remote(most, most, kv_send.at[which], q_recv, sibling).wait_send()
+            remote(most, most, kv_send.at[which], q_send, sibling).wait_send()
     if FLAGS["q"]:
-        pltpu.make_async_copy(q_ref.at[:, columns(my_head)], qbuf.at[my_block // 2, my_sub],
-                              local_sem.at[2]).wait()
         most = q_ref.at[:, pl.ds(0, (PLANE - 1) * HD)]
-        done = remote(most, most, q_send, q_recv, sibling)
-        done.wait_send()
-        done.wait_recv()
-
-    row = lax.broadcasted_iota(jnp.int32, (BLOCK, BLOCK), 0)
-    col = lax.broadcasted_iota(jnp.int32, (BLOCK, BLOCK), 1)
-
-    def attend(zh, logs):
+        remote(most, most, q_send, q_send, sibling).wait_send()
+
+    def turn(n):
+        side = 1 - 2 * (z % 2)
+        step = 2 * ((3 - n) // 3) + side * (3 - 2 * n) * (n * (3 - n) // 2)
+        return (z // 2 + step + OWN) % OWN
+
+    def place(zh):
         i = 2 * zh + core
-        first = doc_ref[y * NB + i]
-        queries = qbuf[zh].reshape(BLOCK, HD)
+        first = docs[y * NB + i]
 
         def where(step):
             j = (i + NB - step) % NB
             plane = (j <= i).astype(jnp.int32)
-            visible = (y + plane - 1) * NB + j >= first
-            return plane, j, visible
-
-        def score(step):
-            plane, j, visible = where(step)
+            return plane, j, (y + plane - 1) * NB + j >= first
+
+        return where
+
+    def multiply_keys(zh, r, s_ref):
+        where = place(zh)
+        queries = qbuf[zh, 2 * r:2 * r + 2].reshape(TILE, HD)
+        for step in range(NB):
+            plane, j, _ = where(step)
             keys = kv[plane, j, :, 0].reshape(BLOCK, HD)
-            return lax.dot_general(queries, keys, (((1,), (1,)), ((), ())),
-                                   preferred_element_type=jnp.float32), visible
-
-        def fold(s):
-            return functools.reduce(jnp.maximum, [s[:, n * HD:(n + 1) * HD] for n in range(BLOCK // HD)])
-
-        home, _ = score(0)
-        home = jnp.where(row >= col, home, -jnp.inf)
-        scores[0] = home
-
-        def first_pass(step, peak):
-            s, visible = score(step)
-            scores[step] = s
-            return jnp.maximum(peak, jnp.where(visible, fold(s), -jnp.inf))
-
-        peak = lax.fori_loop(1, NB, first_pass, fold(home))
-        top = jnp.max(peak, axis=1, keepdims=True)
-
-        def weigh(step, carry):
-            total, value = carry
-            plane, j, visible = where(step)
-            floor = jnp.where(visible, top, jnp.inf)
-            w = jnp.exp((scores[step] - floor) * SCALE).astype(jnp.bfloat16)
-            wide = w.astype(jnp.float32)
-            total = total + functools.reduce(
-                jnp.add, [wide[:, n * HD:(n + 1) * HD] for n in range(BLOCK // HD)])
+            s_ref[:, step * BLOCK:(step + 1) * BLOCK] = lax.dot_general(
+                queries, keys, (((1,), (1,)), ((), ())), preferred_element_type=jnp.float32)
+
+    def weigh(zh, r, s_ref, p_ref, top_ref):
+        where = place(zh)
+        visible = [where(step)[2] for step in range(NB)]
+        for part in range(TILE // PART):
+            here = slice(part * PART, (part + 1) * PART)
+            row = lax.broadcasted_iota(jnp.int32, (PART, HD), 0) + (r * TILE + part * PART)
+            lane = lax.broadcasted_iota(jnp.int32, (PART, HD), 1)
+            home, peak = [], None
+            for step in range(NB):
+                best = None
+                for n in range(BLOCK // HD):
+                    s = s_ref[here, step * BLOCK + n * HD:step * BLOCK + (n + 1) * HD]
+                    if step == 0:
+                        s = jnp.where(row >= lane + n * HD, s, -jnp.inf)
+                        home.append(s)
+                    best = s if best is None else jnp.maximum(best, s)
+                if step > 0:
+                    best = jnp.where(visible[step], best, -jnp.inf)
+                peak = best if peak is None else jnp.maximum(peak, best)
+            top = jnp.broadcast_to(jnp.max(peak, axis=1, keepdims=True), (PART, HD))
+            top_ref[here, :] = top
+            top = top * SCALE2
+            for step in range(NB):
+                floor = top if step == 0 else jnp.where(visible[step], top, jnp.inf)
+                for n in range(BLOCK // HD):
+                    columns_here = slice(step * BLOCK + n * HD, step * BLOCK + (n + 1) * HD)
+                    s = home[n] if step == 0 else s_ref[here, columns_here]
+                    p_ref[here, columns_here] = jnp.exp2(s * SCALE2 - floor).astype(jnp.bfloat16)
+
+    def multiply_values(zh, r, p_ref, top_ref):
+        where = place(zh)
+        both = jnp.zeros((TILE, 2 * HD), jnp.float32)
+        for step in range(NB):
+            plane, j, _ = where(step)
             values = kv[plane, j, :, 1].reshape(BLOCK, HD)
-            value = value + jnp.dot(w, values, preferred_element_type=jnp.float32)
-            return total, value
-
-        zero = jnp.zeros((BLOCK, HD), jnp.float32)
-        total, value = lax.fori_loop(0, NB, weigh, (zero, zero))
-        total = jnp.sum(total, axis=1, keepdims=True)
-        obuf[zh] = (value / total).astype(jnp.bfloat16).reshape(SUBS, ROWS, HD)
-        log_total = top * SCALE + jnp.log(total)
-        lane = lax.broadcasted_iota(jnp.int32, (BLOCK, HD), 1)
-        logs = jnp.where(lane == zh, log_total, logs)
-        if FLAGS["out"]:
-            send_out(zh)
-        return logs
-
-    def send_out(zh):
-        def send(sub, carry):
-            tx, tz = sub // 2, 2 * zh + sub % 2
+            values = jnp.concatenate([values, jnp.ones((BLOCK, HD), jnp.bfloat16)], axis=1)
+            both = both + jnp.dot(p_ref[:, step * BLOCK:(step + 1) * BLOCK], values,
+                                  preferred_element_type=jnp.float32)
+        total = both[:, HD:]
+        obuf[zh, 2 * r:2 * r + 2] = (both[:, :HD] / total).astype(jnp.bfloat16).reshape(2, ROWS, HD)
+        log_total = top_ref[...] * SCALE + jnp.log(total)
+        lse_stage[zh, r:r + 1, :] = jnp.transpose(log_total)[0:1, :]
+
+    def send_out(zh, r):
+        for low in range(2):
+            sub = 2 * r + low
+            tx, tz = r, 2 * zh + low
             here = jnp.logical_and(tx == x, tz == z)
 
             @pl.when(jnp.logical_not(here))
@@ -229,22 +242,51 @@
             def _():
                 pltpu.make_async_copy(obuf.at[zh, sub], out_ref.at[:, columns(my_head)],
                                       local_sem.at[3]).start()
-            return carry
-
-        lax.fori_loop(0, SUBS, send, 0)
-
-    logs = jnp.zeros((BLOCK, HD), jnp.float32)
+
+    def take_q(zh):
+        block = qbuf.at[zh]
+        pltpu.make_async_copy(block, block, q_recv.at[zh]).wait()
+
+    def attend(n, carry):
+        now, before, after = turn(n), turn((n + 3) % 4), turn((n + 1) % 4)
+        for r in range(TILES):
+            s_now, s_next = (s0, s1) if r % 2 == 0 else (s1, s0)
+            p_now, p_last = (p0, p1) if r % 2 == 0 else (p1, p0)
+            top_now, top_last = (top0, top1) if r % 2 == 0 else (top1, top0)
+            if r == TILES - 1:
+                @pl.when(n < OWN - 1)
+                def _():
+                    take_q(after)
+                multiply_keys(after, 0, s_next)
+            else:
+                multiply_keys(now, r + 1, s_next)
+            weigh(now, r, s_now, p_now, top_now)
+            if r == 0:
+                multiply_values(before, TILES - 1, p_last, top_last)
+
+                @pl.when(n > 0)
+                def _():
+                    send_out(before, TILES - 1)
+            else:
+                multiply_values(now, r - 1, p_last, top_last)
+                send_out(now, r - 1)
+        return carry
+
+    fetch_docs.wait()
+    take_q(turn(0))
     if FLAGS["compute"]:
-        logs = lax.fori_loop(0, OWN, attend, logs)
-    elif FLAGS["out"]:
-        lax.fori_loop(0, OWN, lambda zh, c: (send_out(zh), c)[1], 0)
+        multiply_keys(turn(0), 0, s0)
+        lax.fori_loop(0, OWN, attend, 0)
+        multiply_values(turn(OWN - 1), TILES - 1, p1, top1)
+        send_out(turn(OWN - 1), TILES - 1)
+    else:
+        for n in range(1, OWN):
+            take_q(turn(n))
+        for n in range(OWN):
+            for r in range(TILES):
+                send_out(turn(n), r)
 
     if FLAGS["out"]:
-        rows = jnp.transpose(logs)
-        for zh in range(OWN):
-            for n in range(BLOCK // HD):
-                lse_stage[zh, n:n + 1, :] = rows[zh:zh + 1, n * HD:(n + 1) * HD]
-
         def send_logs(zh, carry):
             tz = 2 * zh + z // 4
             here = tz == z
@@ -303,20 +345,26 @@
             jax.ShapeDtypeStruct((ROWS, PLANE * HD), jnp.bfloat16),
             jax.ShapeDtypeStruct((4, BLOCK), jnp.float32),
         ),
-        in_specs=[pl.BlockSpec(memory_space=pltpu.SMEM), any_space, any_space, any_space],
+        in_specs=[any_space] * 4,
         out_specs=(any_space, pl.BlockSpec(memory_space=pltpu.VMEM)),
         scratch_shapes=[
+            pltpu.SMEM((NB * NY,), jnp.int32),
             pltpu.VMEM((OWN, SUBS, ROWS, HD), jnp.bfloat16),
             pltpu.VMEM((2, NB, SUBS, 2, ROWS, HD), jnp.bfloat16),
             pltpu.VMEM((OWN, SUBS, ROWS, HD), jnp.bfloat16),
-            pltpu.VMEM((NB, BLOCK, BLOCK), jnp.float32),
+            pltpu.VMEM((TILE, NB * BLOCK), jnp.float32),
+            pltpu.VMEM((TILE, NB * BLOCK), jnp.float32),
+            pltpu.VMEM((TILE, NB * BLOCK), jnp.bfloat16),
+            pltpu.VMEM((TILE, NB * BLOCK), jnp.bfloat16),
+            pltpu.VMEM((TILE, HD), jnp.float32),
+            pltpu.VMEM((TILE, HD), jnp.float32),
             pltpu.VMEM((OWN, 8, HD), jnp.float32),
             pltpu.VMEM((4, 8, HD), jnp.float32),
-            dma((2,)), dma((PLANE,)), dma, dma, dma, dma, dma, dma((PLANE,)),
+            dma((2,)), dma((PLANE,)), dma, dma((OWN,)), dma, dma, dma, dma((PLANE,)),
             dma, dma, dma, dma, dma((4,)), dma((4,)), dma((5,)),
         ],
         compiler_params=pltpu.CompilerParams(
-            collective_id=0, has_side_effects=True, vmem_limit_bytes=48 * 1024 * 1024,
+            collective_id=0, has_side_effects=True, vmem_limit_bytes=62 * 1024 * 1024,
         ),
         cost_estimate=pl.CostEstimate(flops=17_000_000_000, bytes_accessed=4_000_000, transcendentals=8_400_000),
     )(doc_first, query_rows, key_rows, value_rows)

time: 94.5 us -> 77.2 us (0.82)
  Pallas kernels: 88.4 us -> 73.6 us
  local copies, waits for them, and re-layouts: 5.17 us -> 2.48 us
    pallas_call x1, Pallas kernels: 88.4 us -> 73.6 us  [on_device(): pl.pallas_call(attend_kernel, out_shape=(jax.ShapeDtypeStruct((ROWS, PLAN...]
    unnamed x10 -> x4, local copies, waits for them, and re-layouts: 5.17 us -> 2.48 us
where the time goes in v2:
time: 77.2 us; the launch traced here: 76.7 us
  Pallas kernels  73.6 us (95%)
  local copies, waits for them, and re-layouts  2.48 us (3%)
    pallas_call x1, Pallas kernels, on_device(): pl.pallas_call(attend_kernel, out_shape=(jax.ShapeDtypeStruct((ROWS, PLAN...  73.6 us
    unnamed x4, local copies, waits for them, and re-layouts  2.48 us

profile of v2, /device:TPU:1, one launch (start us, length us, event | category | flops | bytes accessed | tf_op | source)
XLA Modules:
  0.0 76.7 jit_solution(1503690337548890970)
XLA Ops:
  0.6 73.6 %shard_map.59 = (bf16[64,4096]{1,0:T(8,128)(2,1)}, f32[4,512]{1,0:T(4,128)}) custom-call(s32[64]{0:T(128)} %doc_ref.1, bf16[64,4096]{1,0:T(8,128)(2,1)} %q_ref.1, bf16[64,4096]{1,0:T(8,128)(2,1)} %k_ref.1, bf16[64,4096]{1,0:T(8,128)(2,1)} %v_ref.1), custom_call_target="tpu_custom_call" | custom-call | flops 16999999488 | bytes 4000000 | tf_op jit(solution)/shard_map/pallas_call | solution.py:342
  74.2 0.0 copy-start
  74.2 1.9 %copy.8 = bf16[64,4096]{1,0:T(8,128)(2,1)} copy(bf16[64,4096]{1,0:T(8,128)(2,1)} %get-tuple-element.4) | data formatting | bytes 1048576
  76.1 0.0 copy-done
  76.1 0.6 copy.9
Async XLA Ops:
  74.2 1.9 %copy-start = (f32[4,512]{1,0:T(4,128)S(1)}, f32[4,512]{1,0:T(4,128)}, u32[]{:S(2)}) copy-start(f32[4,512]{1,0:T(4,128)} %get-tuple-element.5) | copy-start | bytes 24580

commit v3 on v2

--- a/solution.py
+++ b/solution.py
@@ -88,7 +88,8 @@
         )
 
     if FLAGS["kv"]:
-        def send_kv(t, carry):
+        def send_kv(step, carry):
+            t = PLANE - 2 - step
             device, h = target(t)
             for which, ref in ((0, k_ref), (1, v_ref)):
                 remote(ref.at[:, columns(h)], kv.at[1, my_block, my_sub, which],
@@ -106,7 +107,6 @@
                    q_send, q_recv.at[my_block // 2], device).start()
             return carry
 
-        lax.fori_loop(0, PLANE - 1, send_q, 0)
         pltpu.make_async_copy(q_ref.at[:, columns(my_head)], qbuf.at[my_block // 2, my_sub],
                               q_recv.at[my_block // 2]).start()
 
@@ -116,8 +116,12 @@
     if FLAGS["kv"]:
         def pass_on(t, zh, sub):
             here = chunk(1, zh, core, sub)
+
+            @pl.when(zh + core > 0)
+            def _():
+                remote(here, chunk(0, zh, core, sub), fwd_send, fwd_recv.at[t], ahead).start()
+
             remote(here, here, sib_send, sib_recv, sibling).start()
-            remote(here, chunk(0, zh, core, sub), fwd_send, fwd_recv.at[t], ahead).start()
 
         for which, ref in ((0, k_ref), (1, v_ref)):
             pltpu.make_async_copy(ref.at[:, columns(my_head)], kv.at[1, my_block, my_sub, which],
@@ -125,31 +129,49 @@
         if FLAGS["fwd"]:
             pass_on(PLANE - 1, z // 2, my_sub)
 
-        def take_kv(t, carry):
+        def take_kv(step, carry):
+            t = PLANE - 2 - step
             zh, sub = source(t)
             here = chunk(1, zh, core, sub)
             remote(here, here, kv_send.at[0], kv_recv.at[t], sibling).wait_recv()
             if FLAGS["fwd"]:
                 pass_on(t, zh, sub)
+
+            @pl.when(step >= 19)
+            def _():
+                send_q(step - 19, 0)
+
             return carry
 
         lax.fori_loop(0, PLANE - 1, take_kv, 0)
+        lax.fori_loop(12, PLANE - 1, send_q, 0)
 
     if FLAGS["fwd"]:
-        def take_prev(t, carry):
+        def take_prev(step, carry):
+            t = PLANE - 1 - step
             zh, sub = source(t)
             here = chunk(0, zh, core, sub)
-            remote(here, here, fwd_send, fwd_recv.at[t], sibling).wait_recv()
-            remote(here, here, prev_send, prev_recv, sibling).start()
+
+            @pl.when(zh + core > 0)
+            def _():
+                remote(here, here, fwd_send, fwd_recv.at[t], sibling).wait_recv()
+                remote(here, here, prev_send, prev_recv, sibling).start()
+
             return carry
 
         lax.fori_loop(0, PLANE, take_prev, 0)
         half = kv.at[0, pl.ds(0, OWN)]
-        for send, recv in ((sib_send, sib_recv), (prev_send, prev_recv)):
-            done = remote(half, half, send, recv, sibling)
-            done.wait_send()
-            done.wait_recv()
-        remote(half, half, fwd_send, sib_recv, sibling).wait_send()
+        done = remote(half, half, sib_send, sib_recv, sibling)
+        done.wait_send()
+        done.wait_recv()
+        for parity in range(2):
+            @pl.when(core == parity)
+            def _():
+                sent = kv.at[0, pl.ds(0, OWN - 1 + parity)]
+                remote(sent, sent, fwd_send, prev_recv, sibling).wait_send()
+                remote(sent, sent, prev_send, prev_recv, sibling).wait_send()
+                got = kv.at[0, pl.ds(0, OWN - parity)]
+                remote(got, got, prev_send, prev_recv, sibling).wait_recv()
 
     if FLAGS["kv"]:
         for which, ref in ((0, k_ref), (1, v_ref)):
@@ -227,21 +249,21 @@
         log_total = top_ref[...] * SCALE + jnp.log(total)
         lse_stage[zh, r:r + 1, :] = jnp.transpose(log_total)[0:1, :]
 
-    def send_out(zh, r):
-        for low in range(2):
-            sub = 2 * r + low
-            tx, tz = r, 2 * zh + low
-            here = jnp.logical_and(tx == x, tz == z)
-
-            @pl.when(jnp.logical_not(here))
-            def _():
-                remote(obuf.at[zh, sub], out_ref.at[:, columns(my_head)], o_send, o_recv,
-                       chip_device(y, tx, tz, core)).start()
-
-            @pl.when(here)
-            def _():
-                pltpu.make_async_copy(obuf.at[zh, sub], out_ref.at[:, columns(my_head)],
-                                      local_sem.at[3]).start()
+    def send_out(zh):
+        for r in range(TILES):
+            for low in range(2):
+                source = obuf.at[zh, 2 * r + low]
+                to = out_ref.at[:, columns(my_head)]
+                device = (y * NB + 2 * zh + core, 2 * r + low)
+                mine = jnp.logical_and(zh == z // 2, head == 2 * r + low)
+
+                @pl.when(jnp.logical_not(mine))
+                def _():
+                    remote(source, to, o_send, o_recv, device).start()
+
+                @pl.when(mine)
+                def _():
+                    pltpu.make_async_copy(source, to, local_sem.at[3]).start()
 
     def take_q(zh):
         block = qbuf.at[zh]
@@ -266,10 +288,9 @@
 
                 @pl.when(n > 0)
                 def _():
-                    send_out(before, TILES - 1)
+                    send_out(before)
             else:
                 multiply_values(now, r - 1, p_last, top_last)
-                send_out(now, r - 1)
         return carry
 
     fetch_docs.wait()
@@ -278,13 +299,12 @@
         multiply_keys(turn(0), 0, s0)
         lax.fori_loop(0, OWN, attend, 0)
         multiply_values(turn(OWN - 1), TILES - 1, p1, top1)
-        send_out(turn(OWN - 1), TILES - 1)
+        send_out(turn(OWN - 1))
     else:
         for n in range(1, OWN):
             take_q(turn(n))
         for n in range(OWN):
-            for r in range(TILES):
-                send_out(turn(n), r)
+            send_out(turn(n))
 
     if FLAGS["out"]:
         def send_logs(zh, carry):

time: 77.2 us -> 75.3 us (0.975)
  Pallas kernels: 73.6 us -> 71.4 us
    pallas_call x1, Pallas kernels: 73.6 us -> 71.4 us  [on_device(): pl.pallas_call(attend_kernel, out_shape=(jax.ShapeDtypeStruct((ROWS, PLAN...]
where the time goes in v3:
time: 75.3 us; the launch traced here: 74.5 us
  Pallas kernels  71.4 us (95%)
  local copies, waits for them, and re-layouts  2.48 us (3%)
    pallas_call x1, Pallas kernels, on_device(): pl.pallas_call(attend_kernel, out_shape=(jax.ShapeDtypeStruct((ROWS, PLAN...  71.4 us
    unnamed x4, local copies, waits for them, and re-layouts  2.48 us

profile of v3, /device:TPU:1, one launch (start us, length us, event | category | flops | bytes accessed | tf_op | source)
XLA Modules:
  0.0 74.5 jit_solution(9349082648152623964)
XLA Ops:
  0.6 71.4 %shard_map.59 = (bf16[64,4096]{1,0:T(8,128)(2,1)}, f32[4,512]{1,0:T(4,128)}) custom-call(s32[64]{0:T(128)} %doc_ref.1, bf16[64,4096]{1,0:T(8,128)(2,1)} %q_ref.1, bf16[64,4096]{1,0:T(8,128)(2,1)} %k_ref.1, bf16[64,4096]{1,0:T(8,128)(2,1)} %v_ref.1), custom_call_target="tpu_custom_call" | custom-call | flops 16999999488 | bytes 4000000 | tf_op jit(solution)/shard_map/pallas_call | solution.py:362
  72.1 0.0 copy-start
  72.1 1.9 %copy.8 = bf16[64,4096]{1,0:T(8,128)(2,1)} copy(bf16[64,4096]{1,0:T(8,128)(2,1)} %get-tuple-element.4) | data formatting | bytes 1048576
  73.9 0.0 copy-done
  73.9 0.6 copy.9
Async XLA Ops:
  72.1 1.9 %copy-start = (f32[4,512]{1,0:T(4,128)S(1)}, f32[4,512]{1,0:T(4,128)}, u32[]{:S(2)}) copy-start(f32[4,512]{1,0:T(4,128)} %get-tuple-element.5) | copy-start | bytes 24580

commit v4 on v3

--- a/solution.py
+++ b/solution.py
@@ -249,8 +249,8 @@
         log_total = top_ref[...] * SCALE + jnp.log(total)
         lse_stage[zh, r:r + 1, :] = jnp.transpose(log_total)[0:1, :]
 
-    def send_out(zh):
-        for r in range(TILES):
+    def send_out(zh, tiles):
+        for r in tiles:
             for low in range(2):
                 source = obuf.at[zh, 2 * r + low]
                 to = out_ref.at[:, columns(my_head)]
@@ -288,9 +288,11 @@
 
                 @pl.when(n > 0)
                 def _():
-                    send_out(before)
+                    send_out(before, (2, 3))
             else:
                 multiply_values(now, r - 1, p_last, top_last)
+                if r == 2:
+                    send_out(now, (0, 1))
         return carry
 
     fetch_docs.wait()
@@ -299,12 +301,12 @@
         multiply_keys(turn(0), 0, s0)
         lax.fori_loop(0, OWN, attend, 0)
         multiply_values(turn(OWN - 1), TILES - 1, p1, top1)
-        send_out(turn(OWN - 1))
+        send_out(turn(OWN - 1), (2, 3))
     else:
         for n in range(1, OWN):
             take_q(turn(n))
         for n in range(OWN):
-            send_out(turn(n))
+            send_out(turn(n), range(TILES))
 
     if FLAGS["out"]:
         def send_logs(zh, carry):

time: 75.3 us -> 74.9 us (level)
  Pallas kernels: 71.4 us -> 70.5 us
    pallas_call x1, Pallas kernels: 71.4 us -> 70.5 us  [on_device(): pl.pallas_call(attend_kernel, out_shape=(jax.ShapeDtypeStruct((ROWS, PLAN...]
where the time goes in v4:
time: 74.9 us; the launch traced here: 73.6 us
  Pallas kernels  70.5 us (94%)
  local copies, waits for them, and re-layouts  2.48 us (3%)
    pallas_call x1, Pallas kernels, on_device(): pl.pallas_call(attend_kernel, out_shape=(jax.ShapeDtypeStruct((ROWS, PLAN...  70.5 us
    unnamed x4, local copies, waits for them, and re-layouts  2.48 us

profile of v4, /device:TPU:1, one launch (start us, length us, event | category | flops | bytes accessed | tf_op | source)
XLA Modules:
  0.0 73.6 jit_solution(12810000171975803177)
XLA Ops:
  0.6 70.5 %shard_map.59 = (bf16[64,4096]{1,0:T(8,128)(2,1)}, f32[4,512]{1,0:T(4,128)}) custom-call(s32[64]{0:T(128)} %doc_ref.1, bf16[64,4096]{1,0:T(8,128)(2,1)} %q_ref.1, bf16[64,4096]{1,0:T(8,128)(2,1)} %k_ref.1, bf16[64,4096]{1,0:T(8,128)(2,1)} %v_ref.1), custom_call_target="tpu_custom_call" | custom-call | flops 16999999488 | bytes 4000000 | tf_op jit(solution)/shard_map/pallas_call | solution.py:364
  71.1 0.0 copy-start
  71.1 1.9 %copy.8 = bf16[64,4096]{1,0:T(8,128)(2,1)} copy(bf16[64,4096]{1,0:T(8,128)(2,1)} %get-tuple-element.4) | data formatting | bytes 1048576
  73.0 0.0 copy-done
  73.0 0.6 copy.9
Async XLA Ops:
  71.1 1.9 %copy-start = (f32[4,512]{1,0:T(4,128)S(1)}, f32[4,512]{1,0:T(4,128)}, u32[]{:S(2)}) copy-start(f32[4,512]{1,0:T(4,128)} %get-tuple-element.5) | copy-start | bytes 24580
